TPU v7x, 512 devices: a whole 4x8x8 slice. The times are simulated.
512 devices in a mesh: dap: 128 (over z_lo, y, x, core), dp: 4 (over z_hi).
Axes of the slice: x: 4, y: 8, z: 8 (z_hi: 4, z_lo: 2; z = z_hi * 2 + z_lo), core: 2. Of those that a mesh axis runs over, the one named last changes fastest.
Arguments:
- pair: bfloat16 [1024, 256, 128], P(('dp', 'dap')), parts along dimension 0, may hold values from -6 to 6
- pair_mask: int32 [1024, 256], P(('dp', 'dap')), parts along dimension 0, may hold values from 0 to 1, as said below
- w_left: bfloat16 [128, 256], replicated, may hold values from -0.5 to 0.5
- w_right: bfloat16 [128, 256], replicated, may hold values from -0.5 to 0.5
- w_tri_gate: bfloat16 [128, 128], replicated, may hold values from -0.5 to 0.5
- w_tri_out: bfloat16 [128, 128], replicated, may hold values from -0.5 to 0.5
- w_attend: bfloat16 [128, 512], replicated, may hold values from -0.5 to 0.5
- w_bias: bfloat16 [128, 4], replicated
- w_att_out: bfloat16 [128, 128], replicated, may hold values from -0.5 to 0.5
Outputs:
- pair_out: float32 [1024, 256, 128], P('dp', 'dap'), parts along dimension 0
There are 4 independent parts, one for each index of `dp`. A program takes and returns all parts, laid end to end along the dimension named above; an argument that names none is the same for every part. Nothing has to cross between parts.
Inputs may be any that keep to these rules, and one draw needn't show every extreme that they name: pair_mask[i, i] = 1 for every residue i.
All inputs are finite; a program needn't handle non-finite values.
Results may differ from a plain program's by a relative error of at most 0.014.
The roundings to bfloat16 on the way count: a program that leaves them out, or rounds other values in their place, can miss the bound.
Values may be sent and summed in bfloat16 or wider, within the bound.
A program may use at most 128 MiB of HBM per device.

v0:
```python
import math
import jax
import jax.numpy as jnp
from jax import lax
from jax.sharding import Mesh
from jax.sharding import PartitionSpec as P

DAP = ("dap_0", "dap_1", "dap_2", "dap_3")
DP_DAP = ("dp", "dap_0", "dap_1", "dap_2", "dap_3")


def from_everyone(value, axis):
    length = lax.axis_size(axis)
    return lax.all_to_all(
        jnp.broadcast_to(value[None], (length, *value.shape)), axis, 0, 0, tiled=True
    )


def joined_along(parts, dim):
    parts = jnp.moveaxis(parts, 0, dim)
    dims = parts.shape
    return parts.reshape(*dims[:dim], dims[dim] * dims[dim + 1], *dims[dim + 2 :])


def whole_of(value, axes, dim):
    far, near = axes
    parts = from_everyone(from_everyone(value, far), near)
    return joined_along(parts.swapaxes(0, 1).reshape(-1, *value.shape), dim)


def in_one_piece(arrays, axis, split_dim, concat_dim, along):
    widths = [math.prod(a.shape[along:]) for a in arrays]
    both = jnp.concatenate(
        [a.reshape(*a.shape[:along], w) for a, w in zip(arrays, widths)], axis=along
    )
    result = lax.all_to_all(both, axis, split_axis=split_dim, concat_axis=concat_dim, tiled=True)
    parts = jnp.split(result, [sum(widths[:k]) for k in range(1, len(widths))], axis=along)
    return tuple(
        (b.reshape(*result.shape[:along], *a.shape[along:]) for a, b in zip(arrays, parts))
    )


def layer_norm(x):
    x = x.astype(jnp.float32)
    mean = jnp.mean(x, axis=-1, keepdims=True)
    var = jnp.mean((x - mean) * (x - mean), axis=-1, keepdims=True)
    return (x - mean) / jnp.sqrt(var + 1e-05)


def matmul(x, w):
    flat = x.reshape(-1, x.shape[-1])
    return jnp.dot(flat, w, preferred_element_type=jnp.float32).reshape(
        x.shape[:-1] + (w.shape[1],)
    )


def edges(zn, weight, maskf, hidden):
    both = matmul(zn, weight)
    return (jax.nn.sigmoid(both[..., :hidden]) * both[..., hidden:] * maskf[..., None]).astype(
        jnp.bfloat16
    )


def triangle_update(pair_part, zn_part, tri, w_tri_gate, w_tri_out):
    tn = layer_norm(tri).astype(jnp.bfloat16)
    update = jax.nn.sigmoid(matmul(zn_part, w_tri_gate)) * matmul(tn, w_tri_out)
    return pair_part.astype(jnp.float32) + update


def attention(pair1, mask_cols, w_attend, w_bias, w_att_out):
    inner = w_att_out.shape[0]
    heads = w_bias.shape[1]
    head_dim = inner // heads
    total, local = (pair1.shape[0], pair1.shape[1])
    yn = layer_norm(pair1).astype(jnp.bfloat16)
    proj = matmul(yn, w_attend)
    query = proj[..., :inner].astype(jnp.bfloat16).reshape(total, local, heads, head_dim)
    keys = proj[..., inner : 2 * inner].astype(jnp.bfloat16).reshape(total, local, heads, head_dim)
    values = (
        proj[..., 2 * inner : 3 * inner].astype(jnp.bfloat16).reshape(total, local, heads, head_dim)
    )
    gate = jax.nn.sigmoid(proj[..., 3 * inner :])
    bias_part = jnp.einsum("kic,ch->hki", yn, w_bias, preferred_element_type=jnp.float32).astype(
        jnp.bfloat16
    )
    bias = whole_of(bias_part, (("dap_0", "dap_1", "dap_2"), "dap_3"), 2)
    scores = jnp.einsum(
        "irhd,krhd->rhki", query, keys, preferred_element_type=jnp.float32
    ) / jnp.sqrt(jnp.float32(head_dim))
    scores = scores + bias.astype(jnp.float32)[None]
    live = jnp.transpose(mask_cols.astype(jnp.float32))[:, None, :, None]
    scores = jnp.where(live > 0.5, scores, jnp.float32(-1000000000.0))
    weights = jax.nn.softmax(scores, axis=2).astype(jnp.bfloat16)
    summed = jnp.einsum(
        "rhki,krhd->irhd", weights, values, preferred_element_type=jnp.float32
    ).reshape(total, local, inner)
    att = (gate * summed).astype(jnp.bfloat16)
    return pair1 + matmul(att, w_att_out)


def shards(pair, pair_mask, w_left, w_right, w_tri_gate, w_tri_out, w_attend, w_bias, w_att_out):
    hidden = w_tri_out.shape[0]
    maskf = pair_mask.astype(jnp.float32)
    zn = layer_norm(pair).astype(jnp.bfloat16)
    left_edge = edges(zn, w_left, maskf, hidden)
    right_edge = edges(zn, w_right, maskf, hidden)
    pair_cols, mask_cols = in_one_piece((pair, pair_mask.astype(jnp.bfloat16)), DAP, 1, 0, 2)
    tri = jnp.einsum(
        "ikc,jkc->ijc",
        lax.all_gather(left_edge, DAP, axis=0, tiled=True),
        right_edge,
        preferred_element_type=jnp.float32,
    )
    zn_cols = layer_norm(pair_cols).astype(jnp.bfloat16)
    pair1 = triangle_update(pair_cols, zn_cols, tri, w_tri_gate, w_tri_out)
    return attention(pair1, mask_cols, w_attend, w_bias, w_att_out)


def solution(mesh):
    torus = Mesh(
        mesh.devices.reshape(2, 8, 4, 2, mesh.shape["dp"]),
        ("dap_0", "dap_1", "dap_2", "dap_3", "dp"),
    )
    placed = (P(DP_DAP, None, None), P(DP_DAP, None), P(), P(), P(), P(), P(), P(), P())
    return jax.shard_map(
        shards, mesh=torus, in_specs=placed, out_specs=P("dp", DAP, None), check_vma=False
    )
```

profile of v0, /device:TPU:1, one launch (start us, length us, event | category | flops | bytes accessed | tf_op | source)
XLA Modules:
  0.0 323.6 jit_solution(5676171652191276352)
XLA Ops:
  6.5 1.1 convert_reduce_fusion.1
  7.6 1.2 fusion.18
  8.8 1.2 fusion.39
  10.0 1.2 fusion.41
  11.3 0.8 fusion.21
  12.1 0.0 all-gather.2.cloned.1.call-update
  12.1 0.1 copy.140
  12.3 0.2 copy.141
  12.5 1.0 pad_maximum_fusion
  13.5 14.2 %all-to-all-start = ((bf16[2,256,129]{2,0,1:T(2,128)(2,1)}), bf16[2,256,129]{2,0,1:T(2,128)(2,1)S(1)}, u32[]{:S(2)}, u32[]{:S(2)}) async-start(bf16[2,256,129]{2,0,1:T(2,128)(2,1)} %pad_maximum_fusion), calls=%async_computation | async-start | bytes 524288 | tf_op jit(solution)/shard_map/all_to_all | solution.py:36
  27.7 0.1 copy.146
  27.9 15.0 %all-to-all-done = bf16[2,256,129]{2,0,1:T(2,128)(2,1)S(1)} async-done(((bf16[2,256,129]{2,0,1:T(2,128)(2,1)}), bf16[2,256,129]{2,0,1:T(2,128)(2,1)S(1)}, u32[]{:S(2)}, u32[]{:S(2)}) %all-to-all-start) | async-done | bytes 132128 | tf_op jit(solution)/shard_map/all_to_all | solution.py:36
  42.8 0.2 copy.142
  43.0 0.1 split.8
  43.1 0.1 split.9
  43.2 0.1 copy.172
  43.4 0.1 copy.174
  43.5 0.1 fusion.16
  43.6 0.0 copy-done.6
  43.6 0.3 fusion.5
  43.9 207.1 %all-gather.2.cloned.1.call-done = bf16[256,256,128]{2,1,0:T(8,128)(2,1)} async-done(((bf16[2,256,128]{2,1,0:T(8,128)(2,1)}), bf16[256,256,128]{2,1,0:T(8,128)(2,1)}) %all-gather.2.cloned.1.call-update) | async-done | bytes 16777232 | tf_op jit(solution)/shard_map/all_gather | solution.py:110
  251.0 22.1 %copy.147 = bf16[256,256,128]{1,0,2:T(8,128)(2,1)} copy(bf16[256,256,128]{2,1,0:T(8,128)(2,1)} %all-gather.2.cloned.1.call-done) | data formatting | bytes 33554432 | tf_op jit(solution)/shard_map/all_gather | solution.py:110
  273.1 10.2 %fusion.58 = (f32[256,2]{0,1:T(2,128)S(1)}, f32[256,2,128]{0,1,2:T(2,128)S(1)}) fusion(bf16[2,256,128]{1,0,2:T(2,128)(2,1)S(1)} %copy.146, bf16[256,256,128]{1,0,2:T(8,128)(2,1)} %copy.147), kind=kOutput, calls=%fused_computation.85 | convolution fusion | flops 33619456 | bytes 17172480 | tf_op jit(solution)/shard_map/ikc,jkc->ijc/dot_general | solution.py:108
  283.4 0.2 multiply_reduce_fusion.1
  283.6 0.1 divide_convert_fusion.3
  283.7 0.0 copy-done.2
  283.7 0.2 fusion.59
  284.1 0.1 fusion.6
  284.2 0.8 broadcast_in_dim.13
  285.0 9.0 %all-to-all-start.1 = ((bf16[64,4,256,2]{2,1,3,0:T(4,128)(2,1)}), bf16[64,4,256,2]{2,1,3,0:T(4,128)(2,1)S(1)}, u32[]{:S(2)}, u32[]{:S(2)}) async-start(bf16[64,4,256,2]{2,1,3,0:T(4,128)(2,1)} %broadcast_in_dim.13), calls=%async_computation.1 | async-start | bytes 524288 | tf_op jit(solution)/shard_map/all_to_all | solution.py:14
  294.0 0.3 fusion.60
  294.4 0.1 fusion.56
  294.4 0.1 copy.154
  294.6 0.1 copy.155
  294.7 0.1 copy.152
  294.9 0.1 copy.173
  295.0 9.8 %all-to-all-done.1 = bf16[64,4,256,2]{2,1,3,0:T(4,128)(2,1)S(1)} async-done(((bf16[64,4,256,2]{2,1,3,0:T(4,128)(2,1)}), bf16[64,4,256,2]{2,1,3,0:T(4,128)(2,1)S(1)}, u32[]{:S(2)}, u32[]{:S(2)}) %all-to-all-start.1) | async-done | bytes 262176 | tf_op jit(solution)/shard_map/all_to_all | solution.py:14
  304.8 0.1 broadcast_in_dim.14
  304.9 7.3 %all_to_all.28 = bf16[2,64,4,256,2]{3,2,4,1,0:T(4,128)(2,1)S(1)} all-to-all(bf16[2,64,4,256,2]{3,2,4,1,0:T(4,128)(2,1)S(1)} %broadcast_in_dim.14), channel_id=1, replica_groups=mesh['dap_0'=2,'dap_1'=8,'dap_2'=4,'dap_3'=2,'dp'=4] {'dap_3'}, dimensions={0} | all-to-all | bytes 1048576 | tf_op jit(solution)/shard_map/all_to_all | solution.py:14
  312.2 0.1 convert_bitcast_fusion
  312.4 0.6 copy.157
  312.9 0.3 copy.158
  313.2 0.4 copy.159
  313.6 0.9 fusion.61
  314.5 1.1 fusion.11
  315.6 0.1 fusion.30
  315.7 0.2 convolution_add_fusion
  316.0 0.8 copy.162
  (27 shorter events, 0.3 us)
Async XLA Ops:
  6.5 287.5 %copy-start = (bf16[128,512]{1,0:T(8,128)(2,1)S(1)}, bf16[128,512]{1,0:T(8,128)(2,1)}, u32[]{:S(2)}) copy-start(bf16[128,512]{1,0:T(8,128)(2,1)} %param.15) | copy-start | bytes 393220
  6.5 5.6 %copy-start.1 = (bf16[2,256,128]{2,1,0:T(8,128)(2,1)S(1)}, bf16[2,256,128]{2,1,0:T(8,128)(2,1)}, u32[]{:S(2)}) copy-start(bf16[2,256,128]{2,1,0:T(8,128)(2,1)} %param.9) | copy-start | bytes 393220
  6.5 4.7 %copy-start.4 = (s32[2,256]{1,0:T(2,128)S(1)}, s32[2,256]{1,0:T(2,128)}, u32[]{:S(2)}) copy-start(s32[2,256]{1,0:T(2,128)} %param.10) | copy-start | bytes 6148
  6.5 244.5 %all-gather.2.cloned.1.call-start = ((), (), s32[]{:S(2)}) async-start(), calls=%async_computation.3 | async-start | bytes 16908288 | tf_op jit(solution)/shard_map/all_gather | solution.py:110
  12.1 31.5 %copy-start.6 = (bf16[128,128]{1,0:T(8,128)(2,1)S(1)}, bf16[128,128]{1,0:T(8,128)(2,1)}, u32[]{:S(2)}) copy-start(bf16[128,128]{1,0:T(8,128)(2,1)} %param.13) | copy-start | bytes 98308
  13.5 29.3 %all-to-all-start = ((bf16[2,256,129]{2,0,1:T(2,128)(2,1)}), bf16[2,256,129]{2,0,1:T(2,128)(2,1)S(1)}, u32[]{:S(2)}, u32[]{:S(2)}) async-start(bf16[2,256,129]{2,0,1:T(2,128)(2,1)} %pad_maximum_fusion), calls=%async_computation | async-start | bytes 524288 | tf_op jit(solution)/shard_map/all_to_all | solution.py:36
  273.1 10.6 %copy-start.2 = (bf16[128,128]{1,0:T(8,128)(2,1)S(1)}, bf16[128,128]{1,0:T(8,128)(2,1)}, u32[]{:S(2)}) copy-start(bf16[128,128]{1,0:T(8,128)(2,1)} %param.14) | copy-start | bytes 98308
  283.3 0.7 copy-start.5
  285.0 19.8 %all-to-all-start.1 = ((bf16[64,4,256,2]{2,1,3,0:T(4,128)(2,1)}), bf16[64,4,256,2]{2,1,3,0:T(4,128)(2,1)S(1)}, u32[]{:S(2)}, u32[]{:S(2)}) async-start(bf16[64,4,256,2]{2,1,3,0:T(4,128)(2,1)} %broadcast_in_dim.13), calls=%async_computation.1 | async-start | bytes 524288 | tf_op jit(solution)/shard_map/all_to_all | solution.py:14
  314.5 1.2 copy-start.3
Sparse Core Ops, SparseCore 0:
  12.3 238.7 all-gather.1
where the time goes:
time: 325 us; the launch traced here: 324 us
  waiting for transfers between devices  232 us (71%)
  local copies, waits for them, and re-layouts  26.8 us (8%)
  starting transfers between devices  23.2 us (7%)
  matrix products  15.9 us (5%)
  between operations  13.7 us (4%)
  blocking collectives  7.31 us (2%)
  other arithmetic  4.84 us (1%)
    all_gather x1, waiting for transfers between devices, shards(): lax.all_gather(left_edge, DAP, axis=0, tiled=True)  207 us
    all_gather x1, local copies, waits for them, and re-layouts, shards(): lax.all_gather(left_edge, DAP, axis=0, tiled=True)  22.1 us
    all_to_all x1, waiting for transfers between devices, in_one_piece(): lax.all_to_all(both, axis, split_axis=split_dim, concat_axis=concat_dim,...  15 us
    all_to_all x1, starting transfers between devices, in_one_piece(): lax.all_to_all(both, axis, split_axis=split_dim, concat_axis=concat_dim,...  14.2 us
    dot_general x1, matrix products, shards(): jnp.einsum('ikc,jkc->ijc', lax.all_gather(left_edge, DAP, axis=0, tiled=T...  10.2 us
    all_to_all x1, waiting for transfers between devices, from_everyone(): lax.all_to_all(jnp.broadcast_to(value[None], (length, *value.shape)), axi...  9.77 us
    all_to_all x1, starting transfers between devices, from_everyone(): lax.all_to_all(jnp.broadcast_to(value[None], (length, *value.shape)), axi...  9.02 us
    all_to_all x1, blocking collectives, from_everyone(): lax.all_to_all(jnp.broadcast_to(value[None], (length, *value.shape)), axi...  7.31 us
  transfers between devices with their start and end apart: 3, of which 3 were waited for; matrix products, arithmetic and copies ran while one was open for 1% of the time, Pallas kernels for 0%

commit v1 on v0

--- a/solution.py
+++ b/solution.py
@@ -107,7 +107,9 @@
     pair_cols, mask_cols = in_one_piece((pair, pair_mask.astype(jnp.bfloat16)), DAP, 1, 0, 2)
     tri = jnp.einsum(
         "ikc,jkc->ijc",
-        lax.all_gather(left_edge, DAP, axis=0, tiled=True),
+        jnp.concatenate(
+            lax.all_to_all(jnp.stack([left_edge] * lax.axis_size(DAP)), DAP, 0, 0), axis=0
+        ),
         right_edge,
         preferred_element_type=jnp.float32,
     )

time: 325 us -> 503 us (1.55)
  waiting for transfers between devices: 232 us -> 388 us
  local copies, waits for them, and re-layouts: 26.8 us -> 55.1 us
  between operations: 13.7 us -> 0.36 us
  starting transfers between devices: 23.2 us -> 31.3 us
    all_to_all x0 -> x1, waiting for transfers between devices: none -> 367 us  [shards(): lax.all_to_all(jnp.stack([left_edge] * lax.axis_size(DAP)), DAP, 0, 0)]
    all_gather x1 -> x0, waiting for transfers between devices: 207 us -> none  [shards(): lax.all_gather(left_edge, DAP, axis=0, tiled=True)]
    reshape x0 -> x1, local copies, waits for them, and re-layouts: none -> 24.9 us  [shards(): jnp.concatenate(lax.all_to_all(jnp.stack([left_edge] * lax.axis_size(DAP)...]
    all_gather x1 -> x0, local copies, waits for them, and re-layouts: 22.1 us -> none  [shards(): lax.all_gather(left_edge, DAP, axis=0, tiled=True)]
    all_to_all x0 -> x1, local copies, waits for them, and re-layouts: none -> 14.4 us  [shards(): lax.all_to_all(jnp.stack([left_edge] * lax.axis_size(DAP)), DAP, 0, 0)]
    another operation x0 -> x1, local copies, waits for them, and re-layouts: none -> 10.2 us  [shards(): jnp.stack([left_edge] * lax.axis_size(DAP))]
    all_to_all x0 -> x1, starting transfers between devices: none -> 7.02 us  [shards(): lax.all_to_all(jnp.stack([left_edge] * lax.axis_size(DAP)), DAP, 0, 0)]
where the time goes in v1:
time: 503 us; the launch traced here: 502 us
  waiting for transfers between devices  388 us (77%)
  local copies, waits for them, and re-layouts  55.1 us (11%)
  starting transfers between devices  31.3 us (6%)
  matrix products  15 us (3%)
  blocking collectives  7.32 us (1%)
    all_to_all x1, waiting for transfers between devices, shards(): lax.all_to_all(jnp.stack([left_edge] * lax.axis_size(DAP)), DAP, 0, 0)  367 us
    reshape x1, local copies, waits for them, and re-layouts, shards(): jnp.concatenate(lax.all_to_all(jnp.stack([left_edge] * lax.axis_size(DAP)...  24.9 us
    all_to_all x1, local copies, waits for them, and re-layouts, shards(): lax.all_to_all(jnp.stack([left_edge] * lax.axis_size(DAP)), DAP, 0, 0)  14.4 us
    all_to_all x1, starting transfers between devices, in_one_piece(): lax.all_to_all(both, axis, split_axis=split_dim, concat_axis=concat_dim,...  14.2 us
    all_to_all x1, waiting for transfers between devices, in_one_piece(): lax.all_to_all(both, axis, split_axis=split_dim, concat_axis=concat_dim,...  11 us
    dot_general x1, matrix products, shards(): jnp.einsum('ikc,jkc->ijc', jnp.concatenate(lax.all_to_all(jnp.stack([left...  10.2 us
    another operation x1, local copies, waits for them, and re-layouts, shards(): jnp.stack([left_edge] * lax.axis_size(DAP))  10.2 us
  transfers between devices with their start and end apart: 3, of which 3 were waited for; matrix products, arithmetic and copies ran while one was open for 1% of the time, Pallas kernels for 0%

profile of v1, /device:TPU:1, one launch (start us, length us, event | category | flops | bytes accessed | tf_op | source)
XLA Modules:
  0.0 501.8 jit_solution(2999170607602480266)
XLA Ops:
  0.0 0.8 fusion.57
  0.8 0.2 copy.145
  1.0 1.0 copy.144
  2.0 1.0 pad_maximum_fusion
  3.0 14.2 %all-to-all-start = ((bf16[2,256,129]{2,0,1:T(2,128)(2,1)}), bf16[2,256,129]{2,0,1:T(2,128)(2,1)S(1)}, u32[]{:S(2)}, u32[]{:S(2)}) async-start(bf16[2,256,129]{2,0,1:T(2,128)(2,1)} %pad_maximum_fusion), calls=%async_computation | async-start | bytes 524288 | tf_op jit(solution)/shard_map/all_to_all | solution.py:36
  17.2 1.0 convert_reduce_fusion.1
  18.3 1.2 fusion.18
  19.4 1.2 fusion.39
  20.7 0.3 fusion.41
  21.0 0.2 fusion.21
  21.2 0.1 copy.150
  21.3 11.0 %all-to-all-done = bf16[2,256,129]{2,0,1:T(2,128)(2,1)S(1)} async-done(((bf16[2,256,129]{2,0,1:T(2,128)(2,1)}), bf16[2,256,129]{2,0,1:T(2,128)(2,1)S(1)}, u32[]{:S(2)}, u32[]{:S(2)}) %all-to-all-start) | async-done | bytes 132128 | tf_op jit(solution)/shard_map/all_to_all | solution.py:36
  32.4 10.2 %stack.2 = bf16[128,2,256,128]{2,1,3,0:T(2,128)(2,1)} broadcast(bf16[2,256,128]{1,0,2:T(2,128)(2,1)S(1)} %copy.150), dimensions={1,2,3} | broadcast | bytes 16908288 | tf_op jit(solution)/shard_map/stack | solution.py:111
  42.5 7.0 %all-to-all-start.1 = ((bf16[128,2,256,128]{2,1,3,0:T(2,128)(2,1)}), bf16[128,2,256,128]{2,1,3,0:T(2,128)(2,1)}, u32[]{:S(2)}, u32[]{:S(2)}) async-start(bf16[128,2,256,128]{2,1,3,0:T(2,128)(2,1)} %stack.2), calls=%async_computation.1 | async-start | bytes 33554432 | tf_op jit(solution)/shard_map/all_to_all | solution.py:111
  49.5 0.1 copy.152
  49.7 0.2 copy.146
  49.9 0.1 split.8
  50.0 0.1 split.9
  50.1 0.1 copy.177
  50.2 0.1 copy.179
  50.5 0.3 fusion.5
  50.7 367.1 %all-to-all-done.1 = bf16[128,2,256,128]{2,1,3,0:T(2,128)(2,1)} async-done(((bf16[128,2,256,128]{2,1,3,0:T(2,128)(2,1)}), bf16[128,2,256,128]{2,1,3,0:T(2,128)(2,1)}, u32[]{:S(2)}, u32[]{:S(2)}) %all-to-all-start.1) | async-done | bytes 16777248 | tf_op jit(solution)/shard_map/all_to_all | solution.py:111
  417.8 14.4 %copy.151 = bf16[128,2,256,128]{2,1,0,3:T(2,128)(2,1)} copy(bf16[128,2,256,128]{2,1,3,0:T(2,128)(2,1)} %all-to-all-done.1) | data formatting | bytes 33554432 | tf_op jit(solution)/shard_map/all_to_all | solution.py:111
  432.2 24.9 %reshape.115 = bf16[256,256,128]{1,0,2:T(8,128)(2,1)} reshape(bf16[128,2,256,128]{2,1,0,3:T(2,128)(2,1)} %copy.151) | data formatting | bytes 33554432 | tf_op jit(solution)/shard_map/reshape | solution.py:110
  457.1 10.2 %fusion.58 = (f32[256,2]{0,1:T(2,128)S(1)}, f32[256,2,128]{0,1,2:T(2,128)S(1)}) fusion(bf16[2,256,128]{1,0,2:T(2,128)(2,1)S(1)} %copy.152, bf16[256,256,128]{1,0,2:T(8,128)(2,1)} %reshape.115), kind=kOutput, calls=%fused_computation.85 | convolution fusion | flops 33619456 | bytes 17172480 | tf_op jit(solution)/shard_map/ikc,jkc->ijc/dot_general | solution.py:108
  467.3 0.2 multiply_reduce_fusion.1
  467.5 0.1 divide_convert_fusion.3
  467.7 0.2 fusion.59
  468.1 0.1 fusion.6
  468.2 0.8 broadcast_in_dim.13
  469.0 10.0 %all-to-all-start.2 = ((bf16[64,4,256,2]{2,1,3,0:T(4,128)(2,1)}), bf16[64,4,256,2]{2,1,3,0:T(4,128)(2,1)S(1)}, u32[]{:S(2)}, u32[]{:S(2)}) async-start(bf16[64,4,256,2]{2,1,3,0:T(4,128)(2,1)} %broadcast_in_dim.13), calls=%async_computation.2 | async-start | bytes 524288 | tf_op jit(solution)/shard_map/all_to_all | solution.py:14
  479.0 0.3 fusion.60
  479.4 0.1 copy.159
  479.6 0.1 copy.160
  479.7 0.1 copy.157
  479.8 0.1 copy.178
  480.0 9.8 %all-to-all-done.2 = bf16[64,4,256,2]{2,1,3,0:T(4,128)(2,1)S(1)} async-done(((bf16[64,4,256,2]{2,1,3,0:T(4,128)(2,1)}), bf16[64,4,256,2]{2,1,3,0:T(4,128)(2,1)S(1)}, u32[]{:S(2)}, u32[]{:S(2)}) %all-to-all-start.2) | async-done | bytes 262176 | tf_op jit(solution)/shard_map/all_to_all | solution.py:14
  489.7 0.1 broadcast_in_dim.14
  489.9 7.3 %all_to_all.33 = bf16[2,64,4,256,2]{3,2,4,1,0:T(4,128)(2,1)S(1)} all-to-all(bf16[2,64,4,256,2]{3,2,4,1,0:T(4,128)(2,1)S(1)} %broadcast_in_dim.14), channel_id=1, replica_groups=mesh['dap_0'=2,'dap_1'=8,'dap_2'=4,'dap_3'=2,'dp'=4] {'dap_3'}, dimensions={0} | all-to-all | bytes 1048576 | tf_op jit(solution)/shard_map/all_to_all | solution.py:14
  497.2 0.1 convert_bitcast_fusion
  497.3 0.6 copy.162
  497.9 0.3 copy.163
  498.2 0.4 copy.164
  498.6 0.9 fusion.61
  499.5 1.1 fusion.11
  500.6 0.1 fusion.30
  500.7 0.2 convolution_add_fusion
  500.9 0.8 copy.167
  (29 shorter events, 0.4 us)
Async XLA Ops:
  0.0 479.0 %copy-start = (bf16[128,512]{1,0:T(8,128)(2,1)S(1)}, bf16[128,512]{1,0:T(8,128)(2,1)}, u32[]{:S(2)}) copy-start(bf16[128,512]{1,0:T(8,128)(2,1)} %param.15) | copy-start | bytes 393220
  0.0 20.7 %copy-start.1 = (bf16[2,256,128]{2,1,0:T(8,128)(2,1)S(1)}, bf16[2,256,128]{2,1,0:T(8,128)(2,1)}, u32[]{:S(2)}) copy-start(bf16[2,256,128]{2,1,0:T(8,128)(2,1)} %param.9) | copy-start | bytes 393220
  0.0 20.7 %copy-start.5 = (bf16[128,256]{1,0:T(8,128)(2,1)S(1)}, bf16[128,256]{1,0:T(8,128)(2,1)}, u32[]{:S(2)}) copy-start(bf16[128,256]{1,0:T(8,128)(2,1)} %param.12) | copy-start | bytes 196612
  3.0 29.3 %all-to-all-start = ((bf16[2,256,129]{2,0,1:T(2,128)(2,1)}), bf16[2,256,129]{2,0,1:T(2,128)(2,1)S(1)}, u32[]{:S(2)}, u32[]{:S(2)}) async-start(bf16[2,256,129]{2,0,1:T(2,128)(2,1)} %pad_maximum_fusion), calls=%async_computation | async-start | bytes 524288 | tf_op jit(solution)/shard_map/all_to_all | solution.py:36
  42.5 7.9 %copy-start.6 = (bf16[128,128]{1,0:T(8,128)(2,1)S(1)}, bf16[128,128]{1,0:T(8,128)(2,1)}, u32[]{:S(2)}) copy-start(bf16[128,128]{1,0:T(8,128)(2,1)} %param.13) | copy-start | bytes 98308
  42.5 375.3 %all-to-all-start.1 = ((bf16[128,2,256,128]{2,1,3,0:T(2,128)(2,1)}), bf16[128,2,256,128]{2,1,3,0:T(2,128)(2,1)}, u32[]{:S(2)}, u32[]{:S(2)}) async-start(bf16[128,2,256,128]{2,1,3,0:T(2,128)(2,1)} %stack.2), calls=%async_computation.1 | async-start | bytes 33554432 | tf_op jit(solution)/shard_map/all_to_all | solution.py:111
  457.1 10.6 %copy-start.2 = (bf16[128,128]{1,0:T(8,128)(2,1)S(1)}, bf16[128,128]{1,0:T(8,128)(2,1)}, u32[]{:S(2)}) copy-start(bf16[128,128]{1,0:T(8,128)(2,1)} %param.14) | copy-start | bytes 98308
  467.3 0.7 copy-start.4
  469.0 20.8 %all-to-all-start.2 = ((bf16[64,4,256,2]{2,1,3,0:T(4,128)(2,1)}), bf16[64,4,256,2]{2,1,3,0:T(4,128)(2,1)S(1)}, u32[]{:S(2)}, u32[]{:S(2)}) async-start(bf16[64,4,256,2]{2,1,3,0:T(4,128)(2,1)} %broadcast_in_dim.13), calls=%async_computation.2 | async-start | bytes 524288 | tf_op jit(solution)/shard_map/all_to_all | solution.py:14
  499.5 1.2 copy-start.3
